TPU v7x, 32 devices: a whole 2x2x4 slice. The times are simulated.
32 devices in a mesh: dp: 2 (over y), tensor: 16 (over z, x, core).
Axes of the slice: x: 2, y: 2, z: 4, core: 2. Of those that a mesh axis runs over, the one named last changes fastest.
Arguments:
- hidden_in: bfloat16 [2, 16, 1, 64, 1536], P('dp', 'tensor'), may hold values from -6 to 6
- rotated_queries: bfloat16 [2, 16, 1, 64, 1536], P('dp', 'tensor'), may hold values from -8 to 8
- fresh_key_values: bfloat16 [2, 16, 1, 64, 1024], P('dp', 'tensor'), may hold values from -6 to 6
- cached_key_values: bfloat16 [2, 512, 1024], P('dp', 'tensor'), may hold values from -8 to 8
- cached_len: int32 [2], P('dp'), may hold values from 8 to 512, as said below
- expert_ids: int32 [2, 16, 1, 64, 8], P('dp', 'tensor'), may hold values from 0 to 15, all different within a row; in each aligned block of 64 rows (0 to 63, 64 to 127, ..., all dimensions but the last counted through in order) at most 33 rows name the same one
- route_gates: float32 [2, 16, 1, 64, 8], P('dp', 'tensor'), may hold values from 0.1 to 0.4
- output_weight: bfloat16 [1536, 1536], P('tensor'), may hold values from -3 to 3
- norm_gain: float32 [1536], replicated, may hold values from 0.1 to 1.9
- gate_up: bfloat16 [16, 1536, 1024], P('tensor', 'dp'), may hold values from -0.15625 to 0.15625
- down_weight: bfloat16 [16, 512, 1536], P('tensor', 'dp'), may hold values from -0.25 to 0.25
Outputs:
- hidden_out: bfloat16 [2, 16, 1, 64, 1536], P('dp', 'tensor')
- cache_out: bfloat16 [2, 1536, 1024], P('dp', None, 'tensor')
Inputs may be any that keep to these rules, and one draw needn't show every extreme that they name: `cached_len`: some request has exactly 512 valid slots. `expert_ids`: among the 64 tokens of one device no expert is chosen more than 33 times, and on some device some expert is chosen exactly 33 times.
All inputs are finite; a program needn't handle non-finite values.
Results may differ from a plain program's by a relative error of at most 0.006.
Values may be sent and summed in bfloat16 or wider, within the bound.
A program may use at most 64 MiB of HBM per device.

v0:
```python
import math

import jax
import jax.numpy as jnp
from jax import lax
from jax.sharding import PartitionSpec as P

MODEL_WIDTH = 1536
QUERY_HEADS = 24
KEY_VALUE_HEADS = 8
HEAD_WIDTH = 64
FFE = 512
TOPK = 8


epsilon = 1e-05


def partner_2(block, axis, stride):
    count = lax.axis_size(axis)
    route = []
    for low in range(count):
        high = low | 1 << stride
        if high != low and high < count:
            route += [(low, high), (high, low)]
    return lax.ppermute(block, axis, route)


def joined_rows(blocks, head_fourths, position):
    for which_bit in range(head_fourths.bit_length() - 1):
        partner = partner_2(blocks, "tensor", which_bit)
        low_side = position >> which_bit & 1 == 0
        blocks = jnp.where(
            low_side, jnp.concatenate([blocks, partner], 0), jnp.concatenate([partner, blocks], 0)
        )
    return blocks


def head_layout(local, head_fourths, sub_len):
    request_list, unused_len, heads, last_width = local.shape
    shaped = local.reshape(request_list, head_fourths, sub_len, heads, last_width)
    return jnp.transpose(shaped, (3, 1, 0, 2, 4)).reshape(
        heads * head_fourths, request_list, sub_len, last_width
    )


def attend_request(queries_req, pairs_req, cache_total, length, query_pos):
    row_count = queries_req.shape[0]
    block_rows = math.gcd(row_count, 512)
    block_count = row_count // block_rows
    key_pos = jnp.arange(pairs_req.shape[0], dtype=jnp.int32)
    keys_all = pairs_req[:, :HEAD_WIDTH]
    values_all = pairs_req[:, HEAD_WIDTH:]

    def one_block(packed):
        query_block, pos_block = packed
        scores = lax.dot_general(
            query_block, keys_all, (((1,), (1,)), ((), ())), preferred_element_type=jnp.float32
        ) * (1.0 / math.sqrt(HEAD_WIDTH))
        visible = jnp.where(
            key_pos[None, :] < cache_total,
            key_pos[None, :] < length,
            key_pos[None, :] - cache_total <= pos_block[:, None],
        )
        scores = jnp.where(visible, scores, -1e30)
        highest = jnp.max(scores, 1, keepdims=True)
        weights = jnp.where(visible, jnp.exp(scores - highest), 0.0)
        denoms = jnp.sum(weights, 1, keepdims=True)
        mixed_output = (
            jnp.dot(weights.astype(jnp.bfloat16), values_all, preferred_element_type=jnp.float32)
            / denoms
        )
        return mixed_output.astype(jnp.bfloat16)

    mixed_output = lax.map(
        one_block,
        (
            queries_req.reshape(block_count, block_rows, HEAD_WIDTH),
            query_pos.reshape(block_count, block_rows),
        ),
    )
    return mixed_output.reshape(row_count, HEAD_WIDTH)


def shards(
    hidden_in,
    rotated_queries,
    fresh_key_values,
    cached_key_values,
    cached_len,
    expert_ids,
    route_gates,
    output_weight,
    norm_gain,
    gate_up,
    down_weight,
):
    device_list = lax.axis_size("tensor")
    head_fourths = device_list // KEY_VALUE_HEADS
    query_groups = QUERY_HEADS // KEY_VALUE_HEADS
    request_list = rotated_queries.shape[2]
    request_results = rotated_queries.shape[3]
    cache_row_list = cached_key_values.shape[1]
    partial_rows = request_results // head_fourths
    key_value_width = 2 * HEAD_WIDTH
    cache_total = device_list * cache_row_list
    new_total = device_list * request_results
    position = lax.axis_index("tensor")
    quarter = position % head_fourths
    query_shard = rotated_queries[0, 0].reshape(
        request_list, request_results, KEY_VALUE_HEADS, query_groups * HEAD_WIDTH
    )
    query_send = head_layout(query_shard, head_fourths, partial_rows)
    fresh_shard = fresh_key_values[0, 0].reshape(
        request_list, request_results, KEY_VALUE_HEADS, key_value_width
    )
    cache_shard = cached_key_values.reshape(
        request_list, cache_row_list, KEY_VALUE_HEADS, key_value_width
    )
    fresh_copy = jnp.broadcast_to(
        jnp.transpose(fresh_shard, (2, 0, 1, 3))[:, None],
        (KEY_VALUE_HEADS, head_fourths, request_list, request_results, key_value_width),
    )
    cache_copy = jnp.broadcast_to(
        jnp.transpose(cache_shard, (2, 0, 1, 3))[:, None],
        (KEY_VALUE_HEADS, head_fourths, request_list, cache_row_list, key_value_width),
    )
    pairs_send = jnp.concatenate([cache_copy, fresh_copy], 3).reshape(
        device_list, request_list, cache_row_list + request_results, key_value_width
    )
    query_got, pairs_got = (
        lax.all_to_all(query_send, "tensor", split_axis=0, concat_axis=0, tiled=True),
        lax.all_to_all(pairs_send, "tensor", split_axis=0, concat_axis=0, tiled=True),
    )
    cache_head = jnp.transpose(pairs_got[:, :, :cache_row_list], (1, 0, 2, 3)).reshape(
        request_list, cache_total, key_value_width
    )
    fresh_head = jnp.transpose(pairs_got[:, :, cache_row_list:], (1, 0, 2, 3)).reshape(
        request_list, new_total, key_value_width
    )
    query_pos = (
        jnp.arange(device_list, dtype=jnp.int32)[:, None] * request_results
        + quarter * partial_rows
        + jnp.arange(partial_rows, dtype=jnp.int32)[None, :]
    )
    query_pos = jnp.broadcast_to(
        query_pos[:, :, None], (device_list, partial_rows, query_groups)
    ).reshape(-1)
    col_width = key_value_width // head_fourths
    context = jnp.arange(cache_total + new_total, dtype=jnp.int32)
    length = cached_len[0]
    pairs_req = jnp.concatenate([cache_head[0], fresh_head[0]], 0)
    queries_req = query_got[:, 0].reshape(device_list * partial_rows * query_groups, HEAD_WIDTH)
    attended_all = [
        attend_request(queries_req, pairs_req, cache_total, length, query_pos).reshape(
            device_list, partial_rows, query_groups * HEAD_WIDTH
        )
    ]
    old_cols = lax.dynamic_slice_in_dim(cache_head[0], quarter * col_width, col_width, 1)
    new_cols = lax.dynamic_slice_in_dim(fresh_head[0], quarter * col_width, col_width, 1)
    base_rows = jnp.concatenate([old_cols, jnp.zeros((new_total, col_width), old_cols.dtype)], 0)
    base_rows = jnp.where((context < length)[:, None], base_rows, jnp.zeros_like(base_rows))
    appended_all = [lax.dynamic_update_slice_in_dim(base_rows, new_cols, length, 0)]
    attention_result = jnp.stack(attended_all, 0)
    cache_out = jnp.stack(appended_all, 0)
    head_weight = joined_rows(output_weight[None], head_fourths, position).reshape(
        query_groups * HEAD_WIDTH, MODEL_WIDTH
    )
    head_sums = jnp.dot(
        attention_result.reshape(-1, query_groups * HEAD_WIDTH),
        head_weight,
        preferred_element_type=jnp.float32,
    ).astype(jnp.bfloat16)
    head_sums = jnp.transpose(
        head_sums.reshape(request_list, device_list, partial_rows, MODEL_WIDTH), (1, 0, 2, 3)
    )
    incoming_rows = lax.all_to_all(head_sums, "tensor", split_axis=0, concat_axis=0, tiled=True)
    total_output = jnp.sum(
        incoming_rows.reshape(
            KEY_VALUE_HEADS, head_fourths, request_list, partial_rows, MODEL_WIDTH
        ).astype(jnp.float32),
        0,
    )
    attention_sum = jnp.transpose(total_output, (1, 0, 2, 3)).reshape(
        request_list, request_results, MODEL_WIDTH
    )
    residual = hidden_in[0, 0].astype(jnp.float32) + attention_sum
    meansq = jnp.mean(residual * residual, -1, keepdims=True)
    tokens_dev = request_list * request_results
    normed = (
        (residual * lax.rsqrt(meansq + epsilon) * norm_gain)
        .astype(jnp.bfloat16)
        .reshape(tokens_dev, MODEL_WIDTH)
    )
    capacity = min(
        tokens_dev,
        tokens_dev * TOPK // device_list + max(1, tokens_dev * TOPK // (32 * device_list)),
    )
    ids_flat = expert_ids[0, 0].reshape(-1)
    onehot = (ids_flat[:, None] == jnp.arange(device_list, dtype=jnp.int32)[None, :]).astype(
        jnp.int32
    )
    slot_rank = jnp.sum(onehot * (jnp.cumsum(onehot, 0) - onehot), 1)
    slot_index = ids_flat * capacity + slot_rank
    token_index = jnp.arange(tokens_dev * TOPK, dtype=jnp.int32) // TOPK
    outbound_rows = (
        jnp.zeros((device_list * capacity, MODEL_WIDTH), jnp.bfloat16)
        .at[slot_index]
        .set(normed[token_index])
        .reshape(device_list, capacity, MODEL_WIDTH)
    )
    full_gate_up, full_down = (
        lax.all_gather(gate_up, "dp", axis=1, tiled=True),
        lax.all_gather(down_weight, "dp", axis=1, tiled=True),
    )
    slots_in = lax.all_to_all(outbound_rows, "tensor", split_axis=0, concat_axis=0, tiled=True)
    flat_rows = slots_in.reshape(-1, MODEL_WIDTH)
    hidden_units = jnp.dot(flat_rows, full_gate_up[0], preferred_element_type=jnp.float32)
    active = (jax.nn.silu(hidden_units[:, :FFE]) * hidden_units[:, FFE:]).astype(jnp.bfloat16)
    outputs = jnp.dot(active, full_down[0], preferred_element_type=jnp.float32).astype(jnp.bfloat16)
    computed = outputs.reshape(slots_in.shape)
    returned = lax.all_to_all(computed, "tensor", split_axis=0, concat_axis=0, tiled=True)
    picked = returned.reshape(device_list * capacity, MODEL_WIDTH)[slot_index].reshape(
        tokens_dev, TOPK, MODEL_WIDTH
    )
    gates_local = route_gates[0, 0].reshape(tokens_dev, TOPK)
    mixture = jnp.sum(gates_local[:, :, None] * picked.astype(jnp.float32), 1)
    hidden_out = (
        (residual.reshape(tokens_dev, MODEL_WIDTH) + mixture)
        .astype(jnp.bfloat16)
        .reshape(1, 1, request_list, request_results, MODEL_WIDTH)
    )
    return (hidden_out, cache_out)


def solution(mesh):
    return jax.shard_map(
        shards,
        mesh=mesh,
        in_specs=(
            P("dp", "tensor", None, None, None),
            P("dp", "tensor", None, None, None),
            P("dp", "tensor", None, None, None),
            P("dp", "tensor", None),
            P("dp"),
            P("dp", "tensor", None, None, None),
            P("dp", "tensor", None, None, None),
            P("tensor", None),
            P(),
            P("tensor", "dp", None),
            P("tensor", "dp", None),
        ),
        out_specs=(P("dp", "tensor", None, None, None), P("dp", None, "tensor")),
        check_vma=False,
    )
```

profile of v0, /device:TPU:15, one launch (start us, length us, event | category | flops | bytes accessed | tf_op | source)
XLA Modules:
  0.0 232.4 jit_solution(14951025385957414838)
XLA Ops:
  7.2 1.2 reshape_reshape_squeeze.6
  8.4 0.8 copy.30
  9.1 6.6 %all-to-all-start = ((bf16[16,1,32,192]{3,2,1,0:T(8,128)(2,1)}), bf16[16,1,32,192]{3,2,1,0:T(8,128)(2,1)S(1)}, u32[]{:S(2)}, u32[]{:S(2)}) async-start(bf16[16,1,32,192]{3,2,1,0:T(8,128)(2,1)} %bitcast.2), calls=%async_computation | async-start | bytes 524288 | tf_op jit(solution)/shard_map/all_to_all | solution.py:132
  15.7 1.0 copy.44
  16.9 0.8 pad_maximum_fusion.1
  17.6 6.0 %all-to-all-done = bf16[16,1,32,192]{3,2,1,0:T(8,128)(2,1)S(1)} async-done(((bf16[16,1,32,192]{3,2,1,0:T(8,128)(2,1)}), bf16[16,1,32,192]{3,2,1,0:T(8,128)(2,1)S(1)}, u32[]{:S(2)}, u32[]{:S(2)}) %all-to-all-start) | async-done | bytes 196640 | tf_op jit(solution)/shard_map/all_to_all | solution.py:132
  23.6 5.6 %all-to-all-start.1 = ((bf16[16,1,96,128]{3,2,1,0:T(8,128)(2,1)}), bf16[16,1,96,128]{3,2,1,0:T(8,128)(2,1)S(1)}, u32[]{:S(2)}, u32[]{:S(2)}) async-start(bf16[16,1,96,128]{3,2,1,0:T(8,128)(2,1)} %bitcast.7), calls=%async_computation.1 | async-start | bytes 786432 | tf_op jit(solution)/shard_map/all_to_all | solution.py:133
  29.2 0.4 collective-permute-start
  30.1 0.8 collective-permute-done
  31.0 0.2 reshape_reshape_squeeze.7
  31.2 8.8 %all-to-all-done.1 = bf16[16,1,96,128]{3,2,1,0:T(8,128)(2,1)S(1)} async-done(((bf16[16,1,96,128]{3,2,1,0:T(8,128)(2,1)}), bf16[16,1,96,128]{3,2,1,0:T(8,128)(2,1)S(1)}, u32[]{:S(2)}, u32[]{:S(2)}) %all-to-all-start.1) | async-done | bytes 393248 | tf_op jit(solution)/shard_map/all_to_all | solution.py:133
  40.2 11.6 %while.14 = (s32[]{:T(128)}, bf16[3,512,64]{1,2,0:T(8,128)(2,1)S(1)}, s32[]{:T(128)}, s32[3,512]{1,0:T(4,128)S(1)}, bf16[3,512,64]{2,1,0:T(8,128)(2,1)S(1)}, /*i...) while((s32[]{:T(128)}, bf16[3,512,64]{1,2,0:T(8,128)(2,1)S(1)}, ...), condition=%wide.region_3.4_spmd.clone.clone, body=%wide.region_0.3_spmd.clone.clone.sunk | while | flops 213192192 | bytes 10483813 | solution.py:75
  40.2 0.7 iota_compare_fusion.6
  40.9 1.0 fusion.58
  41.9 1.1 fusion.59
  43.0 1.1 fusion.60
  44.1 0.7 iota_compare_fusion.6
  44.8 1.0 fusion.58
  45.8 1.1 fusion.59
  46.9 1.1 fusion.60
  48.0 0.7 iota_compare_fusion.6
  48.7 1.0 fusion.58
  49.6 1.1 fusion.59
  50.7 1.1 fusion.60
  52.1 0.4 reshape_stack_reshape_reshape.3
  52.4 1.7 convolution_convert_fusion.1
  54.1 5.2 %all-to-all-start.2 = ((bf16[16,1,32,1536]{3,2,1,0:T(8,128)(2,1)}), bf16[16,1,32,1536]{3,2,1,0:T(8,128)(2,1)S(1)}, u32[]{:S(2)}, u32[]{:S(2)}) async-start(bf16[16,1,32,1536]{3,2,1,0:T(8,128)(2,1)} %bitcast.14), calls=%async_computation.2 | async-start | bytes 3145728 | tf_op jit(solution)/shard_map/all_to_all | solution.py:177
  59.6 0.5 all-gather.3.cloned.1.call-update
  60.4 1.2 reduce-window.6
  62.1 33.8 %all-to-all-done.2 = bf16[16,1,32,1536]{3,2,1,0:T(8,128)(2,1)S(1)} async-done(((bf16[16,1,32,1536]{3,2,1,0:T(8,128)(2,1)}), bf16[16,1,32,1536]{3,2,1,0:T(8,128)(2,1)S(1)}, u32[]{:S(2)}, u32[]{:S(2)}) %all-to-all-start.2) | async-done | bytes 1572896 | tf_op jit(solution)/shard_map/all_to_all | solution.py:177
  96.5 8.5 %scatter_custom_fusion = bf16[528,1536]{1,0:T(8,128)(2,1)S(1)} fusion(s32[512]{0:T(512)S(1)} %bitcast.148, bf16[64,1536]{1,0:T(8,128)(2,1)S(1)} %fusion.36, s32[1024]{0:T(1024)S(1)} %pad_clamp_fusion.1, bf16[]{:T(256)} %constant.101.clone.1), kind=kCustom, calls=%fused_computation.31 | custom fusion | bytes 1622018 | tf_op jit(solution)/shard_map/scatter | solution.py:209
  105.0 1.6 reshape.282
  106.6 4.5 %all-to-all-start.3 = ((bf16[16,33,1536]{2,1,0:T(8,128)(2,1)}), bf16[16,33,1536]{2,1,0:T(8,128)(2,1)S(1)}, u32[]{:S(2)}, u32[]{:S(2)}) async-start(bf16[16,33,1536]{2,1,0:T(8,128)(2,1)} %reshape.282), calls=%async_computation.3 | async-start | bytes 3932160 | tf_op jit(solution)/shard_map/all_to_all | solution.py:216
  111.1 0.3 all-gather.5.cloned.1.call-start
  111.3 0.5 all-gather.5.cloned.1.call-update
  111.8 43.9 %all-to-all-done.3 = bf16[16,33,1536]{2,1,0:T(8,128)(2,1)S(1)} async-done(((bf16[16,33,1536]{2,1,0:T(8,128)(2,1)}), bf16[16,33,1536]{2,1,0:T(8,128)(2,1)S(1)}, u32[]{:S(2)}, u32[]{:S(2)}) %all-to-all-start.3) | async-done | bytes 1622048 | tf_op jit(solution)/shard_map/all_to_all | solution.py:216
  155.7 1.5 reshape.283
  157.2 5.6 %fusion.24 = f32[528,1024]{1,0:T(8,128)} fusion(bf16[528,1536]{1,0:T(8,128)(2,1)} %reshape.283, bf16[1,1536,1024]{2,1,0:T(8,128)(2,1)} %all-gather.3.cloned.1.call-done), kind=kOutput, calls=%fused_computation.26 | convolution fusion | flops 1660944384 | bytes 6930432 | tf_op jit(solution)/shard_map/dot_general | solution.py:218
  162.8 3.1 %convolution_convert_fusion = bf16[528,1536]{1,0:T(8,128)(2,1)S(1)} fusion(bf16[1,512,1536]{2,1,0:T(8,128)(2,1)} %all-gather.5.cloned.1.call-done, f32[528,1024]{1,0:T(8,128)} %fusion.24), kind=kOutput, calls=%fused_computation.28 | convolution fusion | flops 832905216 | bytes 5357568 | tf_op jit(solution)/shard_map/dot_general | solution.py:220
  165.9 1.6 reshape.284
  167.4 5.0 %all-to-all-start.4 = ((bf16[16,33,1536]{2,1,0:T(8,128)(2,1)}), bf16[16,33,1536]{2,1,0:T(8,128)(2,1)}, u32[]{:S(2)}, u32[]{:S(2)}) async-start(bf16[16,33,1536]{2,1,0:T(8,128)(2,1)} %reshape.284), calls=%async_computation.4 | async-start | bytes 3932160 | tf_op jit(solution)/shard_map/all_to_all | solution.py:222
  173.7 0.6 dynamic_update_slice.11
  174.3 0.8 copy.41
  175.1 42.1 %all-to-all-done.4 = bf16[16,33,1536]{2,1,0:T(8,128)(2,1)} async-done(((bf16[16,33,1536]{2,1,0:T(8,128)(2,1)}), bf16[16,33,1536]{2,1,0:T(8,128)(2,1)}, u32[]{:S(2)}, u32[]{:S(2)}) %all-to-all-start.4) | async-done | bytes 1622048 | tf_op jit(solution)/shard_map/all_to_all | solution.py:222
  217.2 1.8 reshape.285
  219.0 3.0 %gather_fusion = bf16[512,1536]{1,0:T(8,128)(2,1)} fusion(bf16[528,1536]{1,0:T(8,128)(2,1)S(1)} %reshape.285, s32[1024]{0:T(1024)S(1)} %pad_clamp_fusion), kind=kCustom, calls=%fused_computation.1 | custom fusion | bytes 3147776 | tf_op jit(solution)/shard_map/gather | solution.py:223
  222.0 2.8 %fusion.23 = f32[64,1536]{1,0:T(8,128)S(1)} fusion(bf16[512,1536]{1,0:T(8,128)(2,1)} %gather_fusion, f32[64,8]{1,0:T(8,128)S(1)} %copy.36), kind=kLoop, calls=%fused_computation.24 | loop fusion | flops 2260992 | bytes 1968128 | tf_op jit(solution)/shard_map/reduce_sum | solution.py:227
  224.8 0.7 fusion.37
  (62 shorter events, 3.1 us)
Async XLA Ops:
  7.2 9.6 %copy-start.2 = (bf16[1,32,1024]{2,1,0:T(8,128)(2,1)S(1)}, bf16[1,32,1024]{2,1,0:T(8,128)(2,1)}, u32[]{:S(2)}) copy-start(bf16[1,32,1024]{2,1,0:T(8,128)(2,1)} %param.16) | copy-start | bytes 196612
  9.1 14.5 %all-to-all-start = ((bf16[16,1,32,192]{3,2,1,0:T(8,128)(2,1)}), bf16[16,1,32,192]{3,2,1,0:T(8,128)(2,1)S(1)}, u32[]{:S(2)}, u32[]{:S(2)}) async-start(bf16[16,1,32,192]{3,2,1,0:T(8,128)(2,1)} %bitcast.2), calls=%async_computation | async-start | bytes 524288 | tf_op jit(solution)/shard_map/all_to_all | solution.py:132
  15.7 13.5 %copy-start.1 = (bf16[96,1536]{1,0:T(8,128)(2,1)S(1)}, bf16[96,1536]{1,0:T(8,128)(2,1)}, u32[]{:S(2)}) copy-start(bf16[96,1536]{1,0:T(8,128)(2,1)} %param.20) | copy-start | bytes 884740
  23.6 16.4 %all-to-all-start.1 = ((bf16[16,1,96,128]{3,2,1,0:T(8,128)(2,1)}), bf16[16,1,96,128]{3,2,1,0:T(8,128)(2,1)S(1)}, u32[]{:S(2)}, u32[]{:S(2)}) async-start(bf16[16,1,96,128]{3,2,1,0:T(8,128)(2,1)} %bitcast.7), calls=%async_computation.1 | async-start | bytes 786432 | tf_op jit(solution)/shard_map/all_to_all | solution.py:133
  29.2 1.6 collective-permute-start
  54.1 6.0 %copy-start.3 = (s32[1,1,1,64,8]{3,4,2,1,0:T(8,128)S(1)}, s32[1,1,1,64,8]{3,4,2,1,0:T(8,128)}, u32[]{:S(2)}) copy-start(s32[1,1,1,64,8]{3,4,2,1,0:T(8,128)} %param.18) | copy-start | bytes 6148
  54.1 41.8 %all-to-all-start.2 = ((bf16[16,1,32,1536]{3,2,1,0:T(8,128)(2,1)}), bf16[16,1,32,1536]{3,2,1,0:T(8,128)(2,1)S(1)}, u32[]{:S(2)}, u32[]{:S(2)}) async-start(bf16[16,1,32,1536]{3,2,1,0:T(8,128)(2,1)} %bitcast.14), calls=%async_computation.2 | async-start | bytes 3145728 | tf_op jit(solution)/shard_map/all_to_all | solution.py:177
  59.4 36.8 %copy-start = (bf16[1,1,1,64,1536]{4,3,2,1,0:T(8,128)(2,1)S(1)}, bf16[1,1,1,64,1536]{4,3,2,1,0:T(8,128)(2,1)}, u32[]{:S(2)}) copy-start(bf16[1,1,1,64,1536]{4,3,2,1,0:T(8,128)(2,1)} %param.13) | copy-start | bytes 589828
  59.4 97.8 %all-gather.3.cloned.1.call-start = ((), (), s32[]{:S(2)}) async-start(), calls=%async_computation.5 | async-start | bytes 4718592 | tf_op jit(solution)/shard_map/all_gather | solution.py:213
  60.1 36.2 %copy-start.4 = (f32[1536]{0:T(1024)S(1)}, f32[1536]{0:T(1024)}, u32[]{:S(2)}) copy-start(f32[1536]{0:T(1024)} %param.21) | copy-start | bytes 18436
  106.6 49.1 %all-to-all-start.3 = ((bf16[16,33,1536]{2,1,0:T(8,128)(2,1)}), bf16[16,33,1536]{2,1,0:T(8,128)(2,1)S(1)}, u32[]{:S(2)}, u32[]{:S(2)}) async-start(bf16[16,33,1536]{2,1,0:T(8,128)(2,1)} %reshape.282), calls=%async_computation.3 | async-start | bytes 3932160 | tf_op jit(solution)/shard_map/all_to_all | solution.py:216
  111.1 51.7 %all-gather.5.cloned.1.call-start = ((), (), s32[]{:S(2)}) async-start(), calls=%async_computation.6 | async-start | bytes 2359296 | tf_op jit(solution)/shard_map/all_gather | solution.py:214
  167.4 5.7 %copy-start.5 = (f32[1,1,1,64,8]{3,4,2,1,0:T(8,128)S(1)}, f32[1,1,1,64,8]{3,4,2,1,0:T(8,128)}, u32[]{:S(2)}) copy-start(f32[1,1,1,64,8]{3,4,2,1,0:T(8,128)} %param.19) | copy-start | bytes 6148
  167.4 49.8 %all-to-all-start.4 = ((bf16[16,33,1536]{2,1,0:T(8,128)(2,1)}), bf16[16,33,1536]{2,1,0:T(8,128)(2,1)}, u32[]{:S(2)}, u32[]{:S(2)}) async-start(bf16[16,33,1536]{2,1,0:T(8,128)(2,1)} %reshape.284), calls=%async_computation.4 | async-start | bytes 3932160 | tf_op jit(solution)/shard_map/all_to_all | solution.py:222
Sparse Core Ops, SparseCore 0:
  61.8 44.6 all-gather.2
  113.5 26.8 all-gather.4
where the time goes:
time: 233 us; the launch traced here: 232 us
  waiting for transfers between devices  136 us (58%)
  starting transfers between devices  27.8 us (12%)
  local copies, waits for them, and re-layouts  24.7 us (11%)
  matrix products  16.5 us (7%)
  between operations  15 us (6%)
  other arithmetic  11.9 us (5%)
    all_to_all x1, waiting for transfers between devices, shards(): lax.all_to_all(outbound_rows, 'tensor', split_axis=0, concat_axis=0, tile...  43.9 us
    all_to_all x1, waiting for transfers between devices, shards(): lax.all_to_all(computed, 'tensor', split_axis=0, concat_axis=0, tiled=True)  42.1 us
    all_to_all x1, waiting for transfers between devices, shards(): lax.all_to_all(head_sums, 'tensor', split_axis=0, concat_axis=0, tiled=True)  33.8 us
    all_to_all x1, waiting for transfers between devices, shards(): lax.all_to_all(pairs_send, 'tensor', split_axis=0, concat_axis=0, tiled=T...  8.8 us
    scatter x1, local copies, waits for them, and re-layouts, shards(): outbound_rows = jnp.zeros((device_list * capacity, MODEL_WIDTH), jnp.bflo...  8.52 us
    all_to_all x1, starting transfers between devices, shards(): lax.all_to_all(query_send, 'tensor', split_axis=0, concat_axis=0, tiled=T...  6.55 us
    all_to_all x1, waiting for transfers between devices, shards(): lax.all_to_all(query_send, 'tensor', split_axis=0, concat_axis=0, tiled=T...  6.02 us
    dot_general x1, matrix products, shards(): jnp.dot(flat_rows, full_gate_up[0], preferred_element_type=jnp.float32)  5.59 us
  transfers between devices with their start and end apart: 8, of which 6 were waited for; matrix products, arithmetic and copies ran while one was open for 10% of the time, Pallas kernels for 0%

commit v1 on v0

v1 whole, which is shorter than its diff:
```python
import functools
import math

import jax
import jax.numpy as jnp
from jax import lax
from jax.experimental import pallas as pl
from jax.experimental.pallas import tpu as pltpu
from jax.sharding import PartitionSpec as P

QUERY_HEADS = 24
KEY_VALUE_HEADS = 8
HEAD_WIDTH = 64
FFE = 512

epsilon = 1e-05


def attend(q_ref, cache, fresh, length, base, out_ref):
    tokens = q_ref.shape[0]
    slots, news = cache.shape[0], fresh.shape[0]
    groups = QUERY_HEADS // KEY_VALUE_HEADS
    slot = lax.broadcasted_iota(jnp.int32, (tokens, slots), 1)
    bias_c = jnp.where(slot < length, 0.0, -1e30)[None]
    key = lax.broadcasted_iota(jnp.int32, (tokens, news), 1)
    row = lax.broadcasted_iota(jnp.int32, (tokens, news), 0)
    bias_f = jnp.where(key <= row + base, 0.0, -1e30)[None]
    low = lax.broadcasted_iota(jnp.int32, (tokens, 128), 1) < HEAD_WIDTH
    nt = (((1,), (1,)), ((), ()))
    outs = []
    for h in range(KEY_VALUE_HEADS):
        rows = []
        for g in range(groups):
            i = h * groups + g
            slab = q_ref[:, 128 * (i // 2) : 128 * (i // 2) + 128].astype(jnp.float32) * (
                1.0 / math.sqrt(HEAD_WIDTH)
            )
            if i % 2:
                slab = pltpu.roll(slab, HEAD_WIDTH, 1)
            rows.append(jnp.where(low, slab, 0.0).astype(jnp.bfloat16))
        q = jnp.concatenate(rows, 0)
        kc = cache[:, 128 * h : 128 * h + 128]
        kf = fresh[:, 128 * h : 128 * h + 128]
        sc = lax.dot_general(q, kc, nt, preferred_element_type=jnp.float32)
        sf = lax.dot_general(q, kf, nt, preferred_element_type=jnp.float32)
        sc = sc.reshape(groups, tokens, slots) + bias_c
        sf = sf.reshape(groups, tokens, news) + bias_f
        top = jnp.maximum(jnp.max(sc, -1, keepdims=True), jnp.max(sf, -1, keepdims=True))
        pc = jnp.exp(sc - top)
        pf = jnp.exp(sf - top)
        denoms = jnp.sum(pc, -1, keepdims=True) + jnp.sum(pf, -1, keepdims=True)
        pc = pc.astype(jnp.bfloat16).reshape(groups * tokens, slots)
        pf = pf.astype(jnp.bfloat16).reshape(groups * tokens, news)
        o = jnp.dot(pc, kc, preferred_element_type=jnp.float32) + jnp.dot(
            pf, kf, preferred_element_type=jnp.float32
        )
        o = o.reshape(groups, tokens, 128) / denoms
        outs += [o[g] for g in range(groups)]
        if h % 2:
            for j in range(groups):
                slab = jnp.where(low, pltpu.roll(outs[2 * j], HEAD_WIDTH, 1), outs[2 * j + 1])
                column = 128 * ((h // 2) * groups + j)
                out_ref[:, column : column + 128] = slab.astype(out_ref.dtype)
            outs = []


def attention_kernel(length_ref, q_ref, cache_ref, fresh_ref, out_ref):
    base = lax.axis_index("tensor") * q_ref.shape[0]
    attend(q_ref, cache_ref, fresh_ref, length_ref[0], base, out_ref)


def shards(
    hidden_in,
    rotated_queries,
    fresh_key_values,
    cached_key_values,
    cached_len,
    expert_ids,
    route_gates,
    output_weight,
    norm_gain,
    gate_up,
    down_weight,
):
    n = lax.axis_size("tensor")
    position = lax.axis_index("tensor")
    width = hidden_in.shape[-1]
    tokens = hidden_in.shape[2] * hidden_in.shape[3]
    kvw = fresh_key_values.shape[-1]
    cache_all = lax.all_gather(cached_key_values[0], "tensor", axis=0, tiled=True)
    fresh_all = lax.all_gather(fresh_key_values[0, 0, 0], "tensor", axis=0, tiled=True)
    weight_all = lax.all_gather(output_weight, "tensor", axis=0, tiled=True)
    ids = expert_ids.reshape(tokens, -1)
    gates = route_gates.reshape(tokens, -1)
    dense = jnp.sum(
        jnp.where(ids[:, :, None] == jnp.arange(n, dtype=jnp.int32), gates[:, :, None], 0.0), 1
    )
    dense_all = lax.all_gather(dense, "tensor", axis=0, tiled=True)
    own_gate = lax.dynamic_slice_in_dim(dense_all, position, 1, 1)
    gate_up_all = lax.all_gather(gate_up[0], "dp", axis=0, tiled=True)
    down_all = lax.all_gather(down_weight[0], "dp", axis=0, tiled=True)

    vm = pl.BlockSpec(memory_space=pltpu.VMEM)
    attended = pl.pallas_call(
        attention_kernel,
        out_shape=jax.ShapeDtypeStruct((tokens, width), jnp.bfloat16),
        in_specs=[pl.BlockSpec(memory_space=pltpu.SMEM), vm, vm, vm],
        out_specs=vm,
        compiler_params=pltpu.CompilerParams(vmem_limit_bytes=40 << 20),
        cost_estimate=pl.CostEstimate(
            flops=8 * 10**9, bytes_accessed=4 << 20, transcendentals=3 * 10**6
        ),
    )(cached_len, rotated_queries.reshape(tokens, width), cache_all, fresh_all)
    residual = hidden_in.reshape(tokens, width).astype(jnp.float32) + jnp.dot(
        attended, weight_all, preferred_element_type=jnp.float32
    )
    meansq = jnp.mean(residual * residual, -1, keepdims=True)
    normed = (residual * lax.rsqrt(meansq + epsilon) * norm_gain).astype(jnp.bfloat16)
    normed_all = lax.all_gather(normed, "tensor", axis=0, tiled=True)
    hidden_units = jnp.dot(normed_all, gate_up_all, preferred_element_type=jnp.float32)
    active = (jax.nn.silu(hidden_units[:, :FFE]) * hidden_units[:, FFE:]).astype(jnp.bfloat16)
    outputs = jnp.dot(active, down_all, preferred_element_type=jnp.float32)
    outputs = outputs.astype(jnp.bfloat16).astype(jnp.float32)
    partial = (outputs * own_gate).astype(jnp.bfloat16)
    mixture = lax.psum_scatter(partial, "tensor", scatter_dimension=0, tiled=True)
    hidden_out = (residual + mixture.astype(jnp.float32)).astype(jnp.bfloat16)

    cols = kvw // n
    length = cached_len[0]
    old = lax.dynamic_slice_in_dim(cache_all, position * cols, cols, 1)
    new = lax.dynamic_slice_in_dim(fresh_all, position * cols, cols, 1)
    total = old.shape[0] + new.shape[0]
    rows = jnp.concatenate([old, jnp.zeros_like(new)], 0)
    keep = jnp.arange(total, dtype=jnp.int32) < length
    rows = jnp.where(keep[:, None], rows, jnp.zeros_like(rows))
    cache_out = lax.dynamic_update_slice_in_dim(rows, new, length, 0)[None]
    return hidden_out.reshape(hidden_in.shape), cache_out


def solution(mesh):
    return jax.shard_map(
        shards,
        mesh=mesh,
        in_specs=(
            P("dp", "tensor", None, None, None),
            P("dp", "tensor", None, None, None),
            P("dp", "tensor", None, None, None),
            P("dp", "tensor", None),
            P("dp"),
            P("dp", "tensor", None, None, None),
            P("dp", "tensor", None, None, None),
            P("tensor", None),
            P(),
            P("tensor", "dp", None),
            P("tensor", "dp", None),
        ),
        out_specs=(P("dp", "tensor", None, None, None), P("dp", None, "tensor")),
        check_vma=False,
    )
```

time: 233 us -> 349 us (1.50)
  the two profiles are of different devices: /device:TPU:15 before, /device:TPU:0 now
where the time goes in v1:
time: 349 us
  waiting for transfers between devices  283 us (81%)
  blocking collectives  19.3 us (6%)
  matrix products  17.9 us (5%)
  between operations  14.9 us (4%)
  local copies, waits for them, and re-layouts  6.97 us (2%)
  Pallas kernels  4.65 us (1%)
    reduce_scatter x1, waiting for transfers between devices, shards(): lax.psum_scatter(partial, 'tensor', scatter_dimension=0, tiled=True)  63.2 us
    all_gather x1, waiting for transfers between devices, shards(): normed_all = lax.all_gather(normed, 'tensor', axis=0, tiled=True)  47.9 us
    all_gather x1, waiting for transfers between devices, shards(): weight_all = lax.all_gather(output_weight, 'tensor', axis=0, tiled=True)  45.9 us
    all_gather x1, waiting for transfers between devices, shards(): lax.all_gather(fresh_key_values[0, 0, 0], 'tensor', axis=0, tiled=True)  42.5 us
    all_gather x1, waiting for transfers between devices, shards(): lax.all_gather(cached_key_values[0], 'tensor', axis=0, tiled=True)  40.2 us
    all_gather x1, waiting for transfers between devices, shards(): gate_up_all = lax.all_gather(gate_up[0], 'dp', axis=0, tiled=True)  20.6 us
    all_gather x1, blocking collectives, shards(): dense_all = lax.all_gather(dense, 'tensor', axis=0, tiled=True)  19.3 us
    all_gather x1, waiting for transfers between devices, shards(): down_all = lax.all_gather(down_weight[0], 'dp', axis=0, tiled=True)  19.1 us
  transfers between devices with their start and end apart: 7, of which 7 were waited for; matrix products, arithmetic and copies ran while one was open for 5% of the time, Pallas kernels for 1%

profile of v1, /device:TPU:0, one launch (start us, length us, event | category | flops | bytes accessed | tf_op | source)
XLA Modules:
  0.0 349.0 jit_solution(8440817388240209683)
XLA Ops:
  7.2 0.0 all-gather.16.cloned.1.call-start
  7.2 0.7 all-gather.16.cloned.1.call-update
  7.9 0.0 all-gather.18.cloned.1.call-start
  7.9 0.7 all-gather.18.cloned.1.call-update
  8.6 0.0 all-gather.12.cloned.1.call-start
  8.7 0.7 all-gather.12.cloned.1.call-update
  9.4 0.0 all-gather.20.cloned.1.call-start
  9.4 0.5 all-gather.20.cloned.1.call-update
  10.0 0.0 all-gather.14.cloned.1.call-start
  10.7 40.2 %all-gather.16.cloned.1.call-done = bf16[1,512,1024]{2,1,0:T(8,128)(2,1)} async-done(((bf16[1,32,1024]{2,1,0:T(8,128)(2,1)}), bf16[1,512,1024]{2,1,0:T(8,128)(2,1)}) %all-gather.16.cloned.1.call-update) | async-done | bytes 1048592 | tf_op jit(solution)/shard_map/all_gather | solution.py:90
  50.8 42.5 %all-gather.18.cloned.1.call-done = bf16[1,1,1,1024,1024]{4,3,2,1,0:T(8,128)(2,1)} async-done(((bf16[1,1,1,64,1024]{4,3,2,1,0:T(8,128)(2,1)}), bf16[1,1,1,1024,1024]{4,3,2,1,0:T(8,128)(2,1)}) %all-gather.18.cloned.1.call-update) | async-done | bytes 2097168 | tf_op jit(solution)/shard_map/all_gather | solution.py:91
  93.3 0.0 copy-start
  93.3 1.6 copy-done
  94.9 0.0 copy-start.1
  94.9 1.2 copy-done.1
  96.2 0.9 copy-done.2
  97.1 4.6 %shard_map.122 = bf16[64,1536]{1,0:T(8,128)(2,1)S(1)} custom-call(s32[1]{0:T(128)} %copy.32.length_ref, bf16[64,1536]{1,0:T(8,128)(2,1)S(1)} %bitcast.34, bf16[512,1024]{1,0:T(8,128)(2,1)S(1)} %bitcast.33, bf16[1024,1024]{1,0:T(8,128)(2,1)S(1)} %bitcast.32), custom_call_target="tpu_custom_call" | custom-call | flops 8000000000 | bytes 4194304 | tf_op jit(solution)/shard_map/pallas_call | solution.py:104
  101.7 0.0 copy-start.5
  101.8 0.0 copy-start.6
  101.8 0.0 copy-start.7
  101.8 45.9 %all-gather.12.cloned.1.call-done = bf16[1536,1536]{1,0:T(8,128)(2,1)} async-done(((bf16[96,1536]{1,0:T(8,128)(2,1)}), bf16[1536,1536]{1,0:T(8,128)(2,1)}) %all-gather.12.cloned.1.call-update) | async-done | bytes 4718608 | tf_op jit(solution)/shard_map/all_gather | solution.py:92
  147.7 0.0 copy-done.3
  147.7 3.4 multiply_reduce_fusion
  151.1 0.0 copy-done.5
  151.1 0.8 multiply_convert_fusion.1
  151.9 0.0 all-gather.14.cloned.1.call-update
  151.9 0.0 all-gather.22.cloned.1.call-start
  151.9 0.5 all-gather.22.cloned.1.call-update
  152.5 0.0 reduce-scatter.2.cloned.1.call-start
  152.5 0.0 copy-done.6
  152.5 0.0 copy-done.7
  152.6 19.3 %all-gather.4 = f32[16,64,16]{1,2,0:T(8,128)S(1)} all-gather(f32[1,64,16]{1,2,0:T(8,128)S(1)} %bitcast.37), channel_id=1, replica_groups=mesh['dp'=2,'tensor'=16] {'tensor'}, dimensions={0}, use_global_device_ids=true | all-gather | bytes 69632 | tf_op jit(solution)/shard_map/all_gather | solution.py:98
  171.9 0.1 reshape.41
  172.0 20.6 %all-gather.20.cloned.1.call-done = bf16[1,1536,1024]{2,1,0:T(8,128)(2,1)} async-done(((bf16[1,768,1024]{2,1,0:T(8,128)(2,1)}), bf16[1,1536,1024]{2,1,0:T(8,128)(2,1)}) %all-gather.20.cloned.1.call-update) | async-done | bytes 3145744 | tf_op jit(solution)/shard_map/all_gather | solution.py:100
  192.6 47.9 %all-gather.14.cloned.1.call-done = bf16[1024,1536]{1,0:T(8,128)(2,1)} async-done(((bf16[64,1536]{1,0:T(8,128)(2,1)}), bf16[1024,1536]{1,0:T(8,128)(2,1)}) %all-gather.14.cloned.1.call-update) | async-done | bytes 3145744 | tf_op jit(solution)/shard_map/all_gather | solution.py:119
  240.5 8.3 %fusion = f32[1024,1024]{1,0:T(8,128)} fusion(bf16[1024,1536]{1,0:T(8,128)(2,1)} %all-gather.14.cloned.1.call-done, bf16[1,1536,1024]{2,1,0:T(8,128)(2,1)} %all-gather.20.cloned.1.call-done), kind=kOutput, calls=%fused_computation.2 | convolution fusion | flops 3221225472 | bytes 10485760 | tf_op jit(solution)/shard_map/dot_general | solution.py:120
  248.8 19.1 %all-gather.22.cloned.1.call-done = bf16[1,512,1536]{2,1,0:T(8,128)(2,1)} async-done(((bf16[1,256,1536]{2,1,0:T(8,128)(2,1)}), bf16[1,512,1536]{2,1,0:T(8,128)(2,1)}) %all-gather.22.cloned.1.call-update) | async-done | bytes 1572880 | tf_op jit(solution)/shard_map/all_gather | solution.py:101
  268.0 6.2 %multiply_convert_fusion = bf16[1024,1536]{1,0:T(8,128)(2,1)} fusion(f32[1024]{0:T(1024)S(1)} %bitcast.38, bf16[1,512,1536]{2,1,0:T(8,128)(2,1)} %all-gather.22.cloned.1.call-done, f32[1024,1024]{1,0:T(8,128)} %fusion), kind=kOutput, calls=%fused_computation | convolution fusion | flops 1620049920 | bytes 8916992 | tf_op jit(solution)/shard_map/dot_general | solution.py:122
  274.2 0.0 reduce-scatter.2.cloned.1.call-update
  274.2 1.0 constant_dynamic-slice_fusion.1
  275.3 0.1 copy.29
  275.4 1.1 constant_dynamic-slice_fusion
  276.5 0.1 copy.30
  276.6 0.7 dynamic_update_slice.4
  277.4 0.0 copy-start.4
  277.4 63.2 %reduce-scatter.2.cloned.1.call-done = bf16[64,1536]{1,0:T(8,128)(2,1)} async-done(((bf16[1024,1536]{1,0:T(8,128)(2,1)}), bf16[64,1536]{1,0:T(8,128)(2,1)}) %reduce-scatter.2.cloned.1.call-update) | async-done | bytes 196624 | tf_op jit(solution)/shard_map/reduce_scatter | solution.py:125
  340.6 1.6 fusion.6
  342.2 0.0 copy-done.4
  (8 shorter events, 0.1 us)
Async XLA Ops:
  7.2 43.7 %all-gather.16.cloned.1.call-start = ((), (), s32[]{:S(2)}) async-start(), calls=%async_computation.4 | async-start | bytes 1114112 | tf_op jit(solution)/shard_map/all_gather | solution.py:90
  7.9 85.4 %all-gather.18.cloned.1.call-start = ((), (), s32[]{:S(2)}) async-start(), calls=%async_computation.5 | async-start | bytes 2228224 | tf_op jit(solution)/shard_map/all_gather | solution.py:91
  8.6 139.0 %all-gather.12.cloned.1.call-start = ((), (), s32[]{:S(2)}) async-start(), calls=%async_computation.1 | async-start | bytes 5013504 | tf_op jit(solution)/shard_map/all_gather | solution.py:92
  9.4 183.2 %all-gather.20.cloned.1.call-start = ((), (), s32[]{:S(2)}) async-start(), calls=%async_computation.6 | async-start | bytes 4718592 | tf_op jit(solution)/shard_map/all_gather | solution.py:100
  10.0 230.6 %all-gather.14.cloned.1.call-start = ((), (), s32[]{:S(2)}) async-start(), calls=%async_computation.2 | async-start | bytes 3342336 | tf_op jit(solution)/shard_map/all_gather | solution.py:119
  93.3 1.6 copy-start
  94.9 1.2 copy-start.1
  96.2 0.9 copy-start.2
  97.1 50.6 %copy-start.3 = (bf16[1,1,1,64,1536]{4,3,2,1,0:T(8,128)(2,1)S(1)}, bf16[1,1,1,64,1536]{4,3,2,1,0:T(8,128)(2,1)}, u32[]{:S(2)}) copy-start(bf16[1,1,1,64,1536]{4,3,2,1,0:T(8,128)(2,1)} %param.11) | copy-start | bytes 589828
  101.7 49.3 %copy-start.5 = (f32[1536]{0:T(1024)S(1)}, f32[1536]{0:T(1024)}, u32[]{:S(2)}) copy-start(f32[1536]{0:T(1024)} %param.19) | copy-start | bytes 18436
  101.8 50.8 %copy-start.6 = (f32[1,1,1,64,8]{3,4,2,1,0:T(8,128)S(1)}, f32[1,1,1,64,8]{3,4,2,1,0:T(8,128)}, u32[]{:S(2)}) copy-start(f32[1,1,1,64,8]{3,4,2,1,0:T(8,128)} %param.17) | copy-start | bytes 6148
  101.8 50.8 %copy-start.7 = (s32[1,1,1,64,8]{3,4,2,1,0:T(8,128)S(1)}, s32[1,1,1,64,8]{3,4,2,1,0:T(8,128)}, u32[]{:S(2)}) copy-start(s32[1,1,1,64,8]{3,4,2,1,0:T(8,128)} %param.16) | copy-start | bytes 6148
  151.9 116.1 %all-gather.22.cloned.1.call-start = ((), (), s32[]{:S(2)}) async-start(), calls=%async_computation.7 | async-start | bytes 2359296 | tf_op jit(solution)/shard_map/all_gather | solution.py:101
  152.5 188.1 %reduce-scatter.2.cloned.1.call-start = ((), (), s32[]{:S(2)}) async-start(), calls=%async_computation.3 | async-start | bytes 3342336 | tf_op jit(solution)/shard_map/reduce_scatter | solution.py:125
  277.4 64.8 %copy-start.4 = (bf16[1,1536,64]{1,2,0:T(8,128)(2,1)}, bf16[1,1536,64]{1,2,0:T(8,128)(2,1)S(1)}, u32[]{:S(2)}) copy-start(bf16[1,1536,64]{1,2,0:T(8,128)(2,1)S(1)} %dynamic_update_slice.4) | copy-start | bytes 589828
Sparse Core Ops, SparseCore 0:
  10.2 40.6 all-gather.15
  53.0 40.3 all-gather.17
  95.6 51.9 all-gather.11
  149.1 43.4 all-gather.19
  195.3 45.1 all-gather.13
  241.9 26.0 all-gather.21
  274.3 66.1 reduce-scatter.1

commit v2 on v1

v2 whole, which is shorter than its diff:
```python
import functools
import math

import jax
import jax.numpy as jnp
import numpy as np
from jax import lax
from jax.experimental import pallas as pl
from jax.experimental.pallas import tpu as pltpu
from jax.sharding import PartitionSpec as P

QUERY_HEADS = 24
KEY_VALUE_HEADS = 8
HEAD_WIDTH = 64
FFE = 512

epsilon = 1e-05
CORES = 2
DEPTH = 4
FAR = 1 << 20
MESH = pl.DeviceIdType.MESH


def layer_kernel(
    n,
    n_dp,
    length_ref,
    code_ref,
    q_ref,
    hidden_ref,
    gates_ref,
    gain_ref,
    cache_hbm,
    fresh_hbm,
    weight_hbm,
    gate_up_hbm,
    down_hbm,
    out_ref,
    slab_ref,
    kv,
    wo,
    gu,
    dn,
    tok,
    part,
    from_core,
    from_x,
    from_z,
    attended,
    residual,
    local_sem,
    kv_send,
    kv_recv,
    wo_send,
    wo_recv,
    tok_send,
    tok_recv,
    gu_send,
    gu_recv,
    dn_send,
    dn_recv,
    part_send,
    core_recv,
    x_recv,
    z_recv,
):
    dp = lax.axis_index("dp")
    me = lax.axis_index("tensor")
    wide = n // (DEPTH * CORES)
    z, x, c = me // (wide * CORES), (me // CORES) % wide, me % CORES

    def index(zz, xx, cc):
        return (zz * wide + xx) * CORES + cc

    def z_of(step):
        return (z + step) % DEPTH

    def x_of(step):
        return (x + step) % wide

    other = 1 - c
    core_peer = index(z, x, other)
    z_peers = [index(z_of(s), x, c) for s in range(1, DEPTH)]
    x_peers = [index(z, x_of(s), c) for s in range(1, wide)]
    rows_peers = [(dp + s) % n_dp for s in range(1, n_dp)]

    barrier = pltpu.get_barrier_semaphore()
    for peer in z_peers + x_peers + [core_peer]:
        pl.semaphore_signal(barrier, inc=1, device_id=(dp, peer), device_id_type=MESH)
    for peer in rows_peers:
        pl.semaphore_signal(barrier, inc=1, device_id=(peer, me), device_id_type=MESH)
    cached = cache_hbm.shape[0]
    own = [
        (cache_hbm, kv.at[me, pl.ds(0, cached)]),
        (fresh_hbm, kv.at[me, pl.ds(cached, fresh_hbm.shape[0])]),
        (weight_hbm, wo.at[me]),
        (gate_up_hbm, gu.at[dp]),
        (down_hbm, dn.at[dp]),
    ]
    own = [pltpu.make_async_copy(a, b, local_sem.at[i]) for i, (a, b) in enumerate(own)]
    for copy in own:
        copy.start()
    pl.semaphore_wait(barrier, len(z_peers) + len(x_peers) + 1 + len(rows_peers))

    sent = []

    def push(source, target, send_sem, recv_sem, device):
        copy = pltpu.make_async_remote_copy(
            src_ref=source,
            dst_ref=target,
            send_sem=send_sem,
            recv_sem=recv_sem,
            device_id=device,
            device_id_type=MESH,
        )
        copy.start()
        sent.append(copy)

    def arrived(target, send_sem, recv_sem):
        pltpu.make_async_remote_copy(
            src_ref=target,
            dst_ref=target,
            send_sem=send_sem,
            recv_sem=recv_sem,
            device_id=(dp, core_peer),
            device_id_type=MESH,
        ).wait_recv()

    class Gather:
        def __init__(self, buf, send, recv):
            self.buf, self.send, self.recv, self.used = buf, send, recv, 0

        def to(self, s, peer):
            push(
                self.buf.at[s],
                self.buf.at[s],
                self.send.at[self.used],
                self.recv.at[s],
                (dp, peer),
            )
            self.used += 1

        def wait(self, s):
            arrived(self.buf.at[s], self.send.at[0], self.recv.at[s])

        def begin(self):
            for peer in z_peers + x_peers + [core_peer]:
                self.to(me, peer)

        def forward_z(self, step):
            s = index(z_of(step), x, c)
            self.wait(s)
            for peer in x_peers + [core_peer]:
                self.to(s, peer)

        def forward_x(self, hop, step):
            s = index(z_of(step), x_of(hop), c)
            self.wait(s)
            self.to(s, core_peer)

        def finish_core(self, hop):
            for step in range(DEPTH):
                self.wait(index(z_of(step), x_of(hop), other))

    keys = Gather(kv, kv_send, kv_recv)
    weights = Gather(wo, wo_send, wo_recv)
    own[0].wait()
    own[1].wait()
    keys.begin()
    for i, peer in enumerate(rows_peers):
        push(gate_up_hbm, gu.at[dp], gu_send.at[i], gu_recv.at[dp], (peer, me))
    for i, peer in enumerate(rows_peers):
        push(down_hbm, dn.at[dp], dn_send.at[i], dn_recv.at[dp], (peer, me))
    own[2].wait()
    for step in range(1, DEPTH):
        keys.forward_z(step)
    weights.begin()
    for hop in range(1, wide):
        for step in range(DEPTH):
            keys.forward_x(hop, step)
    for hop in range(wide):
        keys.finish_core(hop)

    tokens, width = q_ref.shape
    total = kv.shape[0] * kv.shape[1]
    groups = QUERY_HEADS // KEY_VALUE_HEADS
    code = jnp.broadcast_to(code_ref[...], (tokens, total))
    row = lax.broadcasted_iota(jnp.int32, (tokens, total), 0) + me * tokens
    limit = jnp.where(code < FAR, row + 1, FAR + length_ref[0])
    bias = jnp.where(code < limit, 0.0, -1e30)[None]
    low = lax.broadcasted_iota(jnp.int32, (tokens, 128), 1) < HEAD_WIDTH
    outs = []
    for h in range(KEY_VALUE_HEADS):
        rows = []
        for g in range(groups):
            i = h * groups + g
            slab = q_ref[:, 128 * (i // 2) : 128 * (i // 2) + 128].astype(jnp.float32) * (
                1.0 / math.sqrt(HEAD_WIDTH)
            )
            if i % 2:
                slab = pltpu.roll(slab, HEAD_WIDTH, 1)
            rows.append(jnp.where(low, slab, 0.0).astype(jnp.bfloat16))
        queries = jnp.concatenate(rows, 0)
        pair = kv[:, :, 128 * h : 128 * h + 128].reshape(total, 128)
        scores = lax.dot_general(
            queries, pair, (((1,), (1,)), ((), ())), preferred_element_type=jnp.float32
        )
        scores = scores.reshape(groups, tokens, total) + bias
        probs = jnp.exp(scores - jnp.max(scores, -1, keepdims=True))
        denoms = jnp.sum(probs, -1, keepdims=True)
        probs_low = probs.astype(jnp.bfloat16).reshape(groups * tokens, total)
        o = jnp.dot(probs_low, pair, preferred_element_type=jnp.float32)
        o = o.reshape(groups, tokens, 128) / denoms
        outs += [o[g] for g in range(groups)]
        if h % 2:
            for j in range(groups):
                slab = jnp.where(low, pltpu.roll(outs[2 * j], HEAD_WIDTH, 1), outs[2 * j + 1])
                column = 128 * ((h // 2) * groups + j)
                attended[:, column : column + 128] = slab.astype(attended.dtype)
            outs = []
            if h // 2 + 1 < DEPTH:
                weights.forward_z(h // 2 + 1)
    lane = pl.multiple_of(me * (kv.shape[2] // n) // 128 * 128, 128)
    slab_ref[...] = kv[:, :, pl.ds(lane, 128)]
    for hop in range(1, wide):
        for step in range(DEPTH):
            weights.forward_x(hop, step)
    for hop in range(wide):
        weights.finish_core(hop)

    projected = jnp.dot(
        attended[...], wo[...].reshape(width, width), preferred_element_type=jnp.float32
    )
    res = hidden_ref[...].astype(jnp.float32) + projected
    residual[...] = res
    meansq = jnp.mean(res * res, -1, keepdims=True)
    tok[me, :, pl.ds(0, width)] = (res * lax.rsqrt(meansq + epsilon) * gain_ref[...]).astype(
        tok.dtype
    )
    tok[me, :, pl.ds(width, 128)] = gates_ref[...]

    normed = Gather(tok, tok_send, tok_recv)
    normed.begin()
    own[3].wait()
    own[4].wait()
    for step in range(1, DEPTH):
        normed.forward_z(step)
    for peer in rows_peers:
        arrived(gu.at[peer], gu_send.at[0], gu_recv.at[peer])
        arrived(dn.at[peer], dn_send.at[0], dn_recv.at[peer])

    def experts(hop, cc):
        blocks = [index(zz, x_of(hop), cc) for zz in range(DEPTH)]
        rows = jnp.concatenate([tok[s, :, pl.ds(0, width)] for s in blocks], 0)
        marks = jnp.concatenate([tok[s, :, pl.ds(width, 128)] for s in blocks], 0)
        lanes = lax.broadcasted_iota(jnp.int32, marks.shape, 1)
        gate = jnp.sum(
            jnp.where((lanes == me) | (lanes == me + n), marks.astype(jnp.float32), 0.0),
            1,
            keepdims=True,
        )
        units = jnp.dot(
            rows, gu[...].reshape(width, 2 * FFE), preferred_element_type=jnp.float32
        )
        first = units[:, :FFE]
        active = (first / (1.0 + jnp.exp(-first)) * units[:, FFE:]).astype(jnp.bfloat16)
        result = jnp.dot(active, dn[...].reshape(FFE, width), preferred_element_type=jnp.float32)
        result = (result.astype(jnp.bfloat16).astype(jnp.float32) * gate).astype(part.dtype)
        for zz, s in enumerate(blocks):
            part[s] = result[zz * tokens : (zz + 1) * tokens]

    used = [0]

    def send_part(s, target, recv_sem, peer):
        push(part.at[s], target, part_send.at[used[0]], recv_sem, (dp, peer))
        used[0] += 1

    def send_core(hop):
        for zz in range(DEPTH):
            s = index(zz, x_of(hop), other)
            slot = zz * wide + x_of(hop)
            send_part(s, from_core.at[slot], core_recv.at[slot], core_peer)

    def add_core(hop, zz):
        s = index(zz, x_of(hop), c)
        slot = zz * wide + x_of(hop)
        arrived(from_core.at[slot], part_send.at[0], core_recv.at[slot])
        return s, part[s].astype(jnp.float32) + from_core[slot].astype(jnp.float32)

    experts(0, c)
    for hop in range(1, wide):
        for step in range(DEPTH):
            normed.forward_x(hop, step)
    normed.finish_core(0)
    experts(0, other)
    send_core(0)
    for hop in range(1, wide):
        normed.finish_core(hop)
        experts(hop, other)
        send_core(hop)
    for hop in range(1, wide):
        experts(hop, c)
        for step in range(DEPTH):
            zz = z_of((step + 1) % DEPTH)
            s, value = add_core(hop, zz)
            part[s] = value.astype(part.dtype)
            slot = (hop - 1) * DEPTH + zz
            send_part(s, from_x.at[slot], x_recv.at[slot], x_peers[hop - 1])

    final = None
    for step in range(DEPTH):
        zz = z_of((step + 1) % DEPTH)
        s, value = add_core(0, zz)
        for hop in range(1, wide):
            slot = (hop - 1) * DEPTH + zz
            arrived(from_x.at[slot], part_send.at[0], x_recv.at[slot])
            value = value + from_x[slot].astype(jnp.float32)
        if step < DEPTH - 1:
            part[s] = value.astype(part.dtype)
            send_part(s, from_z.at[step], z_recv.at[step], z_peers[step])
        else:
            final = residual[...] + value
    for step in range(DEPTH - 1):
        arrived(from_z.at[step], part_send.at[0], z_recv.at[step])
        final = final + from_z[step].astype(jnp.float32)
    out_ref[...] = final.astype(out_ref.dtype)
    for copy in sent:
        copy.wait_send()


def shards(
    hidden_in,
    rotated_queries,
    fresh_key_values,
    cached_key_values,
    cached_len,
    expert_ids,
    route_gates,
    output_weight,
    norm_gain,
    gate_up,
    down_weight,
):
    n = lax.axis_size("tensor")
    position = lax.axis_index("tensor")
    width = hidden_in.shape[-1]
    tokens = hidden_in.shape[2] * hidden_in.shape[3]
    kvw = fresh_key_values.shape[-1]
    ids = expert_ids.reshape(tokens, -1)
    gates = route_gates.reshape(tokens, -1)
    dense = jnp.sum(
        jnp.where(ids[:, :, None] == jnp.arange(n, dtype=jnp.int32), gates[:, :, None], 0.0), 1
    )
    upper = lax.reduce_precision(dense, 8, 7)
    lower = dense - upper
    marks = jnp.concatenate([upper, lower, jnp.zeros((tokens, 128 - 2 * n))], 1)
    marks = marks.astype(jnp.bfloat16)

    n_dp = lax.axis_size("dp")
    slots = cached_key_values.shape[1]
    block = slots + tokens
    code = np.concatenate(
        [
            np.arange(n)[:, None] * slots + np.arange(slots) + FAR,
            np.arange(n)[:, None] * tokens + np.arange(tokens),
        ],
        1,
    ).reshape(1, n * block)
    wide = n // (DEPTH * CORES)
    bf = jnp.bfloat16
    vm = pl.BlockSpec(memory_space=pltpu.VMEM)
    far = pl.BlockSpec(memory_space=pl.ANY)
    dma = pltpu.SemaphoreType.DMA
    hidden_out, slab = pl.pallas_call(
        functools.partial(layer_kernel, n, n_dp),
        out_shape=(
            jax.ShapeDtypeStruct((tokens, width), bf),
            jax.ShapeDtypeStruct((n, block, 128), bf),
        ),
        in_specs=[pl.BlockSpec(memory_space=pltpu.SMEM)] + [vm] * 5 + [far] * 5,
        out_specs=(vm, vm),
        scratch_shapes=[
            pltpu.VMEM((n, block, kvw), bf),
            pltpu.VMEM((n,) + output_weight.shape, bf),
            pltpu.VMEM((n_dp,) + gate_up.shape[1:], bf),
            pltpu.VMEM((n_dp,) + down_weight.shape[1:], bf),
            pltpu.VMEM((n, tokens, width + 128), bf),
            pltpu.VMEM((n, tokens, width), bf),
            pltpu.VMEM((DEPTH * wide, tokens, width), bf),
            pltpu.VMEM((DEPTH * (wide - 1), tokens, width), bf),
            pltpu.VMEM((DEPTH - 1, tokens, width), bf),
            pltpu.VMEM((tokens, width), bf),
            pltpu.VMEM((tokens, width), jnp.float32),
            dma((5,)),
            dma((n,)),
            dma((n,)),
            dma((n,)),
            dma((n,)),
            dma((n,)),
            dma((n,)),
            dma((n_dp,)),
            dma((n_dp,)),
            dma((n_dp,)),
            dma((n_dp,)),
            dma((n,)),
            dma((DEPTH * wide,)),
            dma((DEPTH * (wide - 1),)),
            dma((DEPTH - 1,)),
        ],
        compiler_params=pltpu.CompilerParams(
            collective_id=0, has_side_effects=True, vmem_limit_bytes=56 << 20
        ),
        cost_estimate=pl.CostEstimate(
            flops=10**10, bytes_accessed=8 << 20, transcendentals=4 * 10**6
        ),
    )(
        cached_len,
        jnp.asarray(code, jnp.int32),
        rotated_queries.reshape(tokens, width),
        hidden_in.reshape(tokens, width),
        marks,
        norm_gain.reshape(1, width),
        cached_key_values[0],
        fresh_key_values.reshape(tokens, kvw),
        output_weight,
        gate_up[0],
        down_weight[0],
    )

    cols = kvw // n
    length = cached_len[0]
    mine = lax.dynamic_slice_in_dim(slab, position * cols % 128, cols, 2)
    old = mine[:, :slots].reshape(n * slots, cols)
    new = mine[:, slots:].reshape(n * tokens, cols)
    total = old.shape[0] + new.shape[0]
    rows = jnp.concatenate([old, jnp.zeros_like(new)], 0)
    keep = jnp.arange(total, dtype=jnp.int32) < length
    rows = jnp.where(keep[:, None], rows, jnp.zeros_like(rows))
    cache_out = lax.dynamic_update_slice_in_dim(rows, new, length, 0)[None]
    return hidden_out.reshape(hidden_in.shape), cache_out


def solution(mesh):
    return jax.shard_map(
        shards,
        mesh=mesh,
        in_specs=(
            P("dp", "tensor", None, None, None),
            P("dp", "tensor", None, None, None),
            P("dp", "tensor", None, None, None),
            P("dp", "tensor", None),
            P("dp"),
            P("dp", "tensor", None, None, None),
            P("dp", "tensor", None, None, None),
            P("tensor", None),
            P(),
            P("tensor", "dp", None),
            P("tensor", "dp", None),
        ),
        out_specs=(P("dp", "tensor", None, None, None), P("dp", None, "tensor")),
        check_vma=False,
    )
```

time: 349 us -> 140 us (0.40)
  waiting for transfers between devices: 283 us -> 0 us
  Pallas kernels: 4.65 us -> 131 us
  blocking collectives: 19.3 us -> 0 us
  matrix products: 17.9 us -> 0 us
  between operations: 14.9 us -> 1.41 us
    all_gather x6 -> x0, waiting for transfers between devices: 216 us -> none  [the longest x1 47.9 us: shards(): normed_all = lax.all_gather(normed, 'tensor', axis=0, tiled=True)]
    pallas_call x1, Pallas kernels: 4.65 us -> 131 us  [shards(): pl.pallas_call(functools.partial(layer_kernel, n, n_dp), out_shape=(jax.S...]
    reduce_scatter x1 -> x0, waiting for transfers between devices: 63.2 us -> none  [shards(): lax.psum_scatter(partial, 'tensor', scatter_dimension=0, tiled=True)]
    all_gather x1 -> x0, blocking collectives: 19.3 us -> none  [shards(): dense_all = lax.all_gather(dense, 'tensor', axis=0, tiled=True)]
    dot_general x3 -> x0, matrix products: 17.9 us -> none  [the longest x1 8.31 us: shards(): jnp.dot(normed_all, gate_up_all, preferred_element_type=jnp.float32)]
  transfers between devices with their start and end apart: 7 -> 0, of which waited for: 7 -> 0; matrix products, arithmetic and copies ran while one was open for 5% -> 0% of each run, Pallas kernels for 1% -> 0%
where the time goes in v2:
time: 140 us; the launch traced here: 139 us
  Pallas kernels  131 us (94%)
  local copies, waits for them, and re-layouts  5.4 us (4%)
  other arithmetic  1.45 us (1%)
  between operations  1.41 us (1%)
    pallas_call x1, Pallas kernels, shards(): pl.pallas_call(functools.partial(layer_kernel, n, n_dp), out_shape=(jax.S...  131 us

profile of v2, /device:TPU:0, one launch (start us, length us, event | category | flops | bytes accessed | tf_op | source)
XLA Modules:
  0.0 138.8 jit_solution(11677361646413622358)
XLA Ops:
  0.6 0.7 select_reduce_fusion
  1.4 0.1 copy.22
  1.5 0.1 copy.23
  1.6 0.1 pad.3.clone
  1.6 0.7 maximum_maximum_fusion.gates_ref
  3.0 1.3 reshape.34.gain_ref
  4.3 130.5 %shard_map.131 = (bf16[64,1536]{1,0:T(8,128)(2,1)}, bf16[16,96,128]{2,1,0:T(8,128)(2,1)}) custom-call(s32[1]{0:T(128)} %copy.29.length_ref, s32[1,1536]{1,0:T(1,128)} %constant.32.clone.code_ref, bf16[64,1536]{1,0:T(8,128)(2,1)} %bitcast.25, bf16[64,1536]{1,0:T(8,128)(2,1)} %bitcast.26, bf16[64,128]{1,0:T(8,128)(2,1)} %maximum_maximum_fusion.gates_ref, ...), custom_call_target="tpu_custom_call" | custom-call | flops 10000000000 | bytes 8388608 | tf_op jit(solution)/shard_map/pallas_call | solution.py:374
  134.8 0.0 copy-start
  134.8 1.2 constant_dynamic-slice_fusion.1
  136.0 0.1 copy.26
  136.1 1.0 constant_dynamic-slice_fusion
  137.1 0.1 copy.25
  137.3 0.7 dynamic_update_slice.4
  138.0 0.0 copy-start.1
  138.0 0.0 copy-done
  138.1 0.7 copy.30
  138.8 0.0 copy-done.1
  (5 shorter events, 0.0 us)
Async XLA Ops:
  134.8 3.2 %copy-start = (bf16[64,1536]{1,0:T(8,128)(2,1)S(1)}, bf16[64,1536]{1,0:T(8,128)(2,1)}, u32[]{:S(2)}) copy-start(bf16[64,1536]{1,0:T(8,128)(2,1)} %get-tuple-element.4) | copy-start | bytes 589828
  138.0 0.8 copy-start.1

commit v3 on v2

--- a/solution.py
+++ b/solution.py
@@ -30,15 +30,20 @@
     hidden_ref,
     gates_ref,
     gain_ref,
-    cache_hbm,
-    fresh_hbm,
+    cache_ref,
+    fresh_ref,
     weight_hbm,
     gate_up_hbm,
     down_hbm,
     out_ref,
     slab_ref,
+    kv_out,
+    q_out,
     kv,
+    qs,
     wo,
+    sums,
+    from_plane,
     gu,
     dn,
     tok,
@@ -51,6 +56,10 @@
     local_sem,
     kv_send,
     kv_recv,
+    q_send,
+    q_recv,
+    sums_send,
+    plane_recv,
     wo_send,
     wo_recv,
     tok_send,
@@ -89,17 +98,23 @@
         pl.semaphore_signal(barrier, inc=1, device_id=(dp, peer), device_id_type=MESH)
     for peer in rows_peers:
         pl.semaphore_signal(barrier, inc=1, device_id=(peer, me), device_id_type=MESH)
-    cached = cache_hbm.shape[0]
+    spot = x * CORES + c
     own = [
-        (cache_hbm, kv.at[me, pl.ds(0, cached)]),
-        (fresh_hbm, kv.at[me, pl.ds(cached, fresh_hbm.shape[0])]),
-        (weight_hbm, wo.at[me]),
+        (weight_hbm, wo.at[spot]),
         (gate_up_hbm, gu.at[dp]),
         (down_hbm, dn.at[dp]),
     ]
     own = [pltpu.make_async_copy(a, b, local_sem.at[i]) for i, (a, b) in enumerate(own)]
     for copy in own:
         copy.start()
+    cached, span = cache_ref.shape[0], kv.shape[2]
+    reach = qs.shape[2]
+    for zz in range(DEPTH):
+        kv_out[zz, :cached] = cache_ref[:, zz * span : (zz + 1) * span]
+        kv_out[zz, cached:] = fresh_ref[:, zz * span : (zz + 1) * span]
+        q_out[zz] = q_ref[:, zz * reach : (zz + 1) * reach]
+    kv[me] = kv_out[z]
+    qs[z] = q_out[z]
     pl.semaphore_wait(barrier, len(z_peers) + len(x_peers) + 1 + len(rows_peers))
 
     sent = []
@@ -163,21 +178,43 @@
                 self.wait(index(z_of(step), x_of(hop), other))
 
     keys = Gather(kv, kv_send, kv_recv)
-    weights = Gather(wo, wo_send, wo_recv)
-    own[0].wait()
-    own[1].wait()
-    keys.begin()
+    for step, peer in enumerate(z_peers, 1):
+        push(
+            kv_out.at[z_of(step)],
+            kv.at[me],
+            kv_send.at[keys.used],
+            kv_recv.at[me],
+            (dp, peer),
+        )
+        keys.used += 1
+    for peer in x_peers + [core_peer]:
+        keys.to(me, peer)
+    for step, peer in enumerate(z_peers, 1):
+        push(
+            q_out.at[z_of(step)], qs.at[z], q_send.at[step - 1], q_recv.at[z], (dp, peer)
+        )
     for i, peer in enumerate(rows_peers):
         push(gate_up_hbm, gu.at[dp], gu_send.at[i], gu_recv.at[dp], (peer, me))
     for i, peer in enumerate(rows_peers):
         push(down_hbm, dn.at[dp], dn_send.at[i], dn_recv.at[dp], (peer, me))
-    own[2].wait()
     for step in range(1, DEPTH):
         keys.forward_z(step)
-    weights.begin()
+    own[0].wait()
+    for i, peer in enumerate(x_peers + [core_peer]):
+        push(wo.at[spot], wo.at[spot], wo_send.at[i], wo_recv.at[spot], (dp, peer))
     for hop in range(1, wide):
         for step in range(DEPTH):
             keys.forward_x(hop, step)
+    for hop in range(1, wide):
+        there = x_of(hop) * CORES + c
+        arrived(wo.at[there], wo_send.at[0], wo_recv.at[there])
+        push(
+            wo.at[there],
+            wo.at[there],
+            wo_send.at[wide - 1 + hop],
+            wo_recv.at[there],
+            (dp, core_peer),
+        )
     for hop in range(wide):
         keys.finish_core(hop)
 
@@ -185,53 +222,69 @@
     total = kv.shape[0] * kv.shape[1]
     groups = QUERY_HEADS // KEY_VALUE_HEADS
     code = jnp.broadcast_to(code_ref[...], (tokens, total))
-    row = lax.broadcasted_iota(jnp.int32, (tokens, total), 0) + me * tokens
-    limit = jnp.where(code < FAR, row + 1, FAR + length_ref[0])
-    bias = jnp.where(code < limit, 0.0, -1e30)[None]
     low = lax.broadcasted_iota(jnp.int32, (tokens, 128), 1) < HEAD_WIDTH
-    outs = []
-    for h in range(KEY_VALUE_HEADS):
-        rows = []
-        for g in range(groups):
-            i = h * groups + g
-            slab = q_ref[:, 128 * (i // 2) : 128 * (i // 2) + 128].astype(jnp.float32) * (
-                1.0 / math.sqrt(HEAD_WIDTH)
+
+    def attend(zz):
+        base = index(zz, x, c) * tokens
+        row = lax.broadcasted_iota(jnp.int32, (tokens, total), 0) + base
+        limit = jnp.where(code < FAR, row + 1, FAR + length_ref[0])
+        bias = jnp.where(code < limit, 0.0, -1e30)[None]
+        outs = []
+        for h in range(KEY_VALUE_HEADS // DEPTH):
+            rows = []
+            for g in range(groups):
+                i = h * groups + g
+                slab = qs[zz, :, pl.ds(128 * (i // 2), 128)].astype(jnp.float32) * (
+                    1.0 / math.sqrt(HEAD_WIDTH)
+                )
+                if i % 2:
+                    slab = pltpu.roll(slab, HEAD_WIDTH, 1)
+                rows.append(jnp.where(low, slab, 0.0).astype(jnp.bfloat16))
+            queries = jnp.concatenate(rows, 0)
+            pair = kv[:, :, 128 * h : 128 * h + 128].reshape(total, 128)
+            scores = lax.dot_general(
+                queries, pair, (((1,), (1,)), ((), ())), preferred_element_type=jnp.float32
             )
-            if i % 2:
-                slab = pltpu.roll(slab, HEAD_WIDTH, 1)
-            rows.append(jnp.where(low, slab, 0.0).astype(jnp.bfloat16))
-        queries = jnp.concatenate(rows, 0)
-        pair = kv[:, :, 128 * h : 128 * h + 128].reshape(total, 128)
-        scores = lax.dot_general(
-            queries, pair, (((1,), (1,)), ((), ())), preferred_element_type=jnp.float32
-        )
-        scores = scores.reshape(groups, tokens, total) + bias
-        probs = jnp.exp(scores - jnp.max(scores, -1, keepdims=True))
-        denoms = jnp.sum(probs, -1, keepdims=True)
-        probs_low = probs.astype(jnp.bfloat16).reshape(groups * tokens, total)
-        o = jnp.dot(probs_low, pair, preferred_element_type=jnp.float32)
-        o = o.reshape(groups, tokens, 128) / denoms
-        outs += [o[g] for g in range(groups)]
-        if h % 2:
-            for j in range(groups):
-                slab = jnp.where(low, pltpu.roll(outs[2 * j], HEAD_WIDTH, 1), outs[2 * j + 1])
-                column = 128 * ((h // 2) * groups + j)
-                attended[:, column : column + 128] = slab.astype(attended.dtype)
-            outs = []
-            if h // 2 + 1 < DEPTH:
-                weights.forward_z(h // 2 + 1)
-    lane = pl.multiple_of(me * (kv.shape[2] // n) // 128 * 128, 128)
+            scores = scores.reshape(groups, tokens, total) + bias
+            probs = jnp.exp(scores - jnp.max(scores, -1, keepdims=True))
+            denoms = jnp.sum(probs, -1, keepdims=True)
+            probs_low = probs.astype(jnp.bfloat16).reshape(groups * tokens, total)
+            o = jnp.dot(probs_low, pair, preferred_element_type=jnp.float32)
+            o = o.reshape(groups, tokens, 128) / denoms
+            outs += [o[g] for g in range(groups)]
+        for j in range(len(outs) // 2):
+            slab = jnp.where(low, pltpu.roll(outs[2 * j], HEAD_WIDTH, 1), outs[2 * j + 1])
+            attended[:, 128 * j : 128 * j + 128] = slab.astype(attended.dtype)
+
+    def projected():
+        return jnp.dot(
+            attended[...], wo[...].reshape(reach, width), preferred_element_type=jnp.float32
+        )
+
+    for step in range(1, DEPTH):
+        zz = z_of(step)
+        arrived(qs.at[zz], q_send.at[0], q_recv.at[zz])
+        attend(zz)
+        if step == 1:
+            for hop in range(wide):
+                there = x_of(hop) * CORES + other
+                arrived(wo.at[there], wo_send.at[0], wo_recv.at[there])
+        sums[step - 1] = projected().astype(sums.dtype)
+        push(
+            sums.at[step - 1],
+            from_plane.at[step - 1],
+            sums_send.at[step - 1],
+            plane_recv.at[step - 1],
+            (dp, z_peers[step - 1]),
+        )
+    attend(z)
+    lane = pl.multiple_of(me * (span * DEPTH // n) // 128 * 128 - z * span, 128)
     slab_ref[...] = kv[:, :, pl.ds(lane, 128)]
-    for hop in range(1, wide):
-        for step in range(DEPTH):
-            weights.forward_x(hop, step)
-    for hop in range(wide):
-        weights.finish_core(hop)
-
-    projected = jnp.dot(
-        attended[...], wo[...].reshape(width, width), preferred_element_type=jnp.float32
-    )
-    res = hidden_ref[...].astype(jnp.float32) + projected
+
+    res = hidden_ref[...].astype(jnp.float32) + projected()
+    for step in range(DEPTH - 1):
+        arrived(from_plane.at[step], sums_send.at[0], plane_recv.at[step])
+        res = res + from_plane[step].astype(jnp.float32)
     residual[...] = res
     meansq = jnp.mean(res * res, -1, keepdims=True)
     tok[me, :, pl.ds(0, width)] = (res * lax.rsqrt(meansq + epsilon) * gain_ref[...]).astype(
@@ -241,8 +294,8 @@
 
     normed = Gather(tok, tok_send, tok_recv)
     normed.begin()
-    own[3].wait()
-    own[4].wait()
+    own[1].wait()
+    own[2].wait()
     for step in range(1, DEPTH):
         normed.forward_z(step)
     for peer in rows_peers:
@@ -377,11 +430,16 @@
             jax.ShapeDtypeStruct((tokens, width), bf),
             jax.ShapeDtypeStruct((n, block, 128), bf),
         ),
-        in_specs=[pl.BlockSpec(memory_space=pltpu.SMEM)] + [vm] * 5 + [far] * 5,
+        in_specs=[pl.BlockSpec(memory_space=pltpu.SMEM)] + [vm] * 7 + [far] * 3,
         out_specs=(vm, vm),
         scratch_shapes=[
-            pltpu.VMEM((n, block, kvw), bf),
-            pltpu.VMEM((n,) + output_weight.shape, bf),
+            pltpu.VMEM((DEPTH, block, kvw // DEPTH), bf),
+            pltpu.VMEM((DEPTH, tokens, width // DEPTH), bf),
+            pltpu.VMEM((n, block, kvw // DEPTH), bf),
+            pltpu.VMEM((DEPTH, tokens, width // DEPTH), bf),
+            pltpu.VMEM((n // DEPTH,) + output_weight.shape, bf),
+            pltpu.VMEM((DEPTH - 1, tokens, width), bf),
+            pltpu.VMEM((DEPTH - 1, tokens, width), bf),
             pltpu.VMEM((n_dp,) + gate_up.shape[1:], bf),
             pltpu.VMEM((n_dp,) + down_weight.shape[1:], bf),
             pltpu.VMEM((n, tokens, width + 128), bf),
@@ -389,11 +447,15 @@
             pltpu.VMEM((DEPTH * wide, tokens, width), bf),
             pltpu.VMEM((DEPTH * (wide - 1), tokens, width), bf),
             pltpu.VMEM((DEPTH - 1, tokens, width), bf),
-            pltpu.VMEM((tokens, width), bf),
+            pltpu.VMEM((tokens, width // DEPTH), bf),
             pltpu.VMEM((tokens, width), jnp.float32),
-            dma((5,)),
-            dma((n,)),
-            dma((n,)),
+            dma((3,)),
+            dma((n,)),
+            dma((n,)),
+            dma((DEPTH - 1,)),
+            dma((DEPTH,)),
+            dma((DEPTH - 1,)),
+            dma((DEPTH - 1,)),
             dma((n,)),
             dma((n,)),
             dma((n,)),

time: 140 us -> 116 us (0.83)
  Pallas kernels: 131 us -> 107 us
    pallas_call x1, Pallas kernels: 131 us -> 107 us  [shards(): pl.pallas_call(functools.partial(layer_kernel, n, n_dp), out_shape=(jax.S...]
where the time goes in v3:
time: 116 us; the launch traced here: 115 us
  Pallas kernels  107 us (92%)
  local copies, waits for them, and re-layouts  5.4 us (5%)
  other arithmetic  1.45 us (1%)
  between operations  1.41 us (1%)
    pallas_call x1, Pallas kernels, shards(): pl.pallas_call(functools.partial(layer_kernel, n, n_dp), out_shape=(jax.S...  107 us

profile of v3, /device:TPU:0, one launch (start us, length us, event | category | flops | bytes accessed | tf_op | source)
XLA Modules:
  0.0 114.8 jit_solution(8776872530004119612)
XLA Ops:
  0.6 0.7 select_reduce_fusion
  1.4 0.1 copy.22
  1.5 0.1 copy.23
  1.6 0.1 pad.3.clone
  1.6 0.7 maximum_maximum_fusion.gates_ref
  3.0 1.3 %reshape.34.gain_ref = f32[1,1536]{1,0:T(1,128)} reshape(f32[1536]{0:T(1024)} %param.20) | data formatting | bytes 12288 | tf_op jit(solution)/shard_map/reshape | solution.py:484
  4.3 106.5 %shard_map.131 = (bf16[64,1536]{1,0:T(8,128)(2,1)}, bf16[16,96,128]{2,1,0:T(8,128)(2,1)}) custom-call(s32[1]{0:T(128)} %copy.29.length_ref, s32[1,1536]{1,0:T(1,128)} %constant.32.clone.code_ref, bf16[64,1536]{1,0:T(8,128)(2,1)} %bitcast.25, bf16[64,1536]{1,0:T(8,128)(2,1)} %bitcast.26, bf16[64,128]{1,0:T(8,128)(2,1)} %maximum_maximum_fusion.gates_ref, ...), custom_call_target="tpu_custom_call" | custom-call | flops 10000000000 | bytes 8388608 | tf_op jit(solution)/shard_map/pallas_call | solution.py:427
  110.8 0.0 copy-start
  110.8 1.2 %constant_dynamic-slice_fusion.1 = bf16[16,64,64]{2,1,0:T(8,128)(2,1)S(1)} fusion(bf16[16,96,128]{2,1,0:T(8,128)(2,1)} %get-tuple-element.5, s32[]{:T(128)S(6)} %add.15, s32[]{:T(128)S(6)} %select_n.23), kind=kLoop, calls=%fused_computation.7 | loop fusion | bytes 262152 | tf_op jit(solution)/shard_map/slice | solution.py:496
  112.0 0.1 copy.26
  112.1 1.0 constant_dynamic-slice_fusion
  113.2 0.1 copy.25
  113.3 0.7 dynamic_update_slice.4
  114.0 0.0 copy-start.1
  114.1 0.0 copy-done
  114.1 0.7 copy.30
  114.8 0.0 copy-done.1
  (5 shorter events, 0.0 us)
Async XLA Ops:
  110.8 3.2 %copy-start = (bf16[64,1536]{1,0:T(8,128)(2,1)S(1)}, bf16[64,1536]{1,0:T(8,128)(2,1)}, u32[]{:S(2)}) copy-start(bf16[64,1536]{1,0:T(8,128)(2,1)} %get-tuple-element.4) | copy-start | bytes 589828
  114.0 0.8 copy-start.1
